TPU v7x, 32 devices: a whole 2x2x4 slice. The times are simulated.
32 devices in a mesh: group: 2 (over x), segment: 8 (over z, y), tensor: 2 (over core).
Axes of the slice: x: 2, y: 2, z: 4, core: 2. Of those that a mesh axis runs over, the one named last changes fastest.
Arguments:
- stream_in: bfloat16 [64, 8192], P('group', 'tensor'), parts along dimension 0, may hold values from -6 to 6
- cache_k: bfloat16 [8, 512, 16, 1024], P('segment', 'group', None, 'tensor'), parts along dimension 1, may hold values from -7 to 7
- cache_v: bfloat16 [8, 512, 16, 1024], P('segment', 'group', None, 'tensor'), parts along dimension 1, may hold values from -6 to 6
- new_k: bfloat16 [8, 64, 1024], P('segment', 'group', 'tensor'), parts along dimension 1, may hold values from -6 to 6
- new_v: bfloat16 [8, 64, 1024], P('segment', 'group', 'tensor'), parts along dimension 1, may hold values from -6 to 6
- q_gain: bfloat16 [8, 8192], P('segment', 'tensor'), may hold values from 0.25 to 1.75
- page_table: int32 [64, 8], P('group'), parts along dimension 0, may hold values from 0 to 255, as said below
- lengths: int32 [64], P('group'), parts along dimension 0, may hold values from 1 to 128, as said below
Outputs:
- streams: bfloat16 [8, 64, 8192], P('segment', 'group', 'tensor'), parts along dimension 1
- replica_k: bfloat16 [8, 64, 16, 1024], P('segment', 'group', None, 'tensor'), parts along dimension 1
- replica_v: bfloat16 [8, 64, 16, 1024], P('segment', 'group', None, 'tensor'), parts along dimension 1
There are 2 independent parts, one for each index of `group`. A program takes and returns all parts, laid end to end along the dimension named above; an argument that names none is the same for every part. Nothing has to cross between parts.
Inputs may be any that keep to these rules, and one draw needn't show every extreme that they name: `page_table`: each part's page table holds every pool page exactly once. `lengths`: about half of the rows end on a page boundary; some row holds the full 8 * 16 tokens.
All inputs are finite; a program needn't handle non-finite values.
Results may differ from a plain program's by a relative error of at most 0.012.
Values may be sent and summed in bfloat16 or wider, within the bound.
A program may use at most 64 MiB of HBM per device.

v0:
```python
import jax
import jax.numpy as jnp
from jax import lax
from jax.sharding import PartitionSpec as P

HEAD_DIM = 128
PAGE = 16


EPSILON = 1e-06


def from_behind(x, axis, by):
    peers = lax.axis_size(axis)
    return lax.ppermute(x, axis, [(i, (i + by) % peers) for i in range(peers)])


def from_behind_2(value, axis, steps):
    count = lax.axis_size(axis)
    leading, last = (max(0, -steps), min(count, count - steps))
    return lax.ppermute(value, axis, [(source, source + steps) for source in range(leading, last)])


def section_attention(
    current, keys_pool, values_pool, fresh_key, fresh_value, gain, table_rows, row_lengths
):
    rows = current.shape[0]
    width = current.shape[1]
    heads_here = width // HEAD_DIM
    kv_here = keys_pool.shape[-1] // HEAD_DIM
    group_size = heads_here // kv_here
    context = table_rows.shape[1] * PAGE
    widened = current.astype(jnp.float32).reshape(rows, heads_here, HEAD_DIM)
    mean_square = jnp.mean(widened * widened, axis=-1, keepdims=True)
    query = (
        widened
        * lax.rsqrt(mean_square + EPSILON)
        * gain.astype(jnp.float32).reshape(heads_here, HEAD_DIM)
    ).astype(jnp.bfloat16)
    query = query.reshape(rows, kv_here, group_size, HEAD_DIM)
    keys = keys_pool[table_rows].reshape(rows, context, kv_here, HEAD_DIM)
    values = values_pool[table_rows].reshape(rows, context, kv_here, HEAD_DIM)
    fresh_k = fresh_key.reshape(rows, kv_here, HEAD_DIM)
    fresh_v = fresh_value.reshape(rows, kv_here, HEAD_DIM).astype(jnp.float32)
    score_scale = HEAD_DIM ** (-0.5)
    scores = (
        jnp.einsum("rkgd,rtkd->rkgt", query, keys, preferred_element_type=jnp.float32) * score_scale
    )
    own_score = (
        jnp.einsum("rkgd,rkd->rkg", query, fresh_k, preferred_element_type=jnp.float32)
        * score_scale
    )
    visible = (jnp.arange(context)[None, :] < row_lengths[:, None])[:, None, None, :]
    scores = jnp.where(visible, scores, -1e30)
    highest = jnp.maximum(jnp.max(scores, axis=-1), own_score)
    weights = jnp.where(visible, jnp.exp(scores - highest[..., None]), 0.0)
    own_weight = jnp.exp(own_score - highest)
    denominator = jnp.sum(weights, axis=-1) + own_weight
    weights = (weights / denominator[..., None]).astype(jnp.bfloat16)
    own_weight = (own_weight / denominator).astype(jnp.bfloat16).astype(jnp.float32)
    mixed = jnp.einsum("rkgt,rtkd->rkgd", weights, values, preferred_element_type=jnp.float32)
    mixed = mixed + own_weight[..., None] * fresh_v[:, :, None, :]
    return (current.astype(jnp.float32) + mixed.reshape(rows, width)).astype(jnp.bfloat16)


def completed_pages(pool, page_table, lengths):
    finished = lengths % PAGE == 0
    last_page = jnp.maximum(lengths // PAGE - 1, 0)
    page_ids = jnp.take_along_axis(page_table, last_page[:, None], axis=1)[:, 0]
    picked = pool[page_ids]
    return jnp.where(finished[:, None, None], picked, jnp.zeros_like(picked))


def shards(stream_in, cache_k, cache_v, new_k, new_v, q_gain, page_table, lengths):
    section = lax.axis_index("segment")
    sections = lax.axis_size("segment")
    keys_pool = cache_k[0]
    values_pool = cache_v[0]
    fresh_keys = new_k[0]
    fresh_values = new_v[0]
    gain = q_gain[0]
    all_rows = stream_in.shape[0]
    width_here = stream_in.shape[1]
    own_k = completed_pages(keys_pool, page_table, lengths)
    own_v = completed_pages(values_pool, page_table, lengths)
    block_count = all_rows // all_rows
    turns = sections + block_count - 1

    def advance(turn, received):
        offset = turn - section
        active = jnp.logical_and(offset >= 0, offset < block_count)
        first_row = jnp.clip(offset, 0, block_count - 1) * all_rows
        current = jnp.where(section == 0, stream_in, received)
        result = section_attention(
            current, keys_pool, values_pool, fresh_keys, fresh_values, gain, page_table, lengths
        )
        return (active, first_row, result)

    def record(buffer, active, result):
        return jnp.where(active, result, buffer)

    buffer = jnp.zeros((all_rows, width_here), jnp.bfloat16)
    received = jnp.zeros((all_rows, width_here), jnp.bfloat16)
    replica_k, replica_v = from_behind((own_k, own_v), "segment", 1)
    first_turn = 0

    def loop_turn(turn, carried):
        incoming, stored = carried
        active, first_row, result = advance(turn, incoming)
        stored = record(stored, active, result)
        outgoing = from_behind_2(result, "segment", 1)
        return (outgoing, stored)

    received, buffer = lax.fori_loop(first_turn, turns, loop_turn, (received, buffer))
    return (buffer[None], replica_k[None], replica_v[None])


def solution(mesh):
    in_specs = (
        P("group", "tensor"),
        P("segment", "group", None, "tensor"),
        P("segment", "group", None, "tensor"),
        P("segment", "group", "tensor"),
        P("segment", "group", "tensor"),
        P("segment", "tensor"),
        P("group", None),
        P("group"),
    )
    out_specs = (
        P("segment", "group", "tensor"),
        P("segment", "group", None, "tensor"),
        P("segment", "group", None, "tensor"),
    )
    return jax.shard_map(shards, mesh=mesh, in_specs=in_specs, out_specs=out_specs, check_vma=False)
```

profile of v0, /device:TPU:16, one launch (start us, length us, event | category | flops | bytes accessed | tf_op | source)
XLA Modules:
  0.0 195.8 jit_solution(12373279136790922516)
XLA Ops:
  0.6 0.7 fusion.24
  1.3 0.7 fusion.26
  2.0 1.4 gather_fusion.4
  3.4 0.7 fusion.25
  4.1 2.8 %gather_fusion.2 = bf16[32,16,512]{2,1,0:T(8,128)(2,1)S(1)} fusion(bf16[256,16,512]{2,1,0:T(8,128)(2,1)} %bitcast.88, s32[1024]{0:T(1024)S(1)} %pad_clamp_fusion), kind=kCustom, calls=%fused_computation.3 | custom fusion | bytes 1048704 | tf_op jit(solution)/shard_map/gather | solution.py:70
  6.9 2.8 %gather_fusion.3 = bf16[32,16,512]{2,1,0:T(8,128)(2,1)S(1)} fusion(bf16[256,16,512]{2,1,0:T(8,128)(2,1)} %bitcast.86, s32[1024]{0:T(1024)S(1)} %pad_clamp_fusion), kind=kCustom, calls=%fused_computation.4 | custom fusion | bytes 1048704 | tf_op jit(solution)/shard_map/gather | solution.py:70
  9.8 1.6 collective-permute-start.1
  11.4 1.5 collective-permute-start.2
  13.1 5.0 %gather_fusion.1 = bf16[256,16,512]{2,1,0:T(8,128)(2,1)} fusion(bf16[256,16,512]{2,1,0:T(8,128)(2,1)} %bitcast.87, s32[1024]{0:T(1024)S(1)} %pad_clamp_fusion.1), kind=kCustom, calls=%fused_computation.2 | custom fusion | bytes 8389632 | tf_op jit(solution)/shard_map/while/body/eval_jaxpr/gather | solution.py:42
  18.1 4.9 %gather_fusion = bf16[256,16,512]{2,1,0:T(8,128)(2,1)} fusion(bf16[256,16,512]{2,1,0:T(8,128)(2,1)} %bitcast.89, s32[1024]{0:T(1024)S(1)} %pad_clamp_fusion.1), kind=kCustom, calls=%fused_computation.1 | custom fusion | bytes 8389632 | tf_op jit(solution)/shard_map/while/body/eval_jaxpr/gather | solution.py:41
  23.1 6.9 %reshape.223 = bf16[32,128,4,128]{3,2,1,0:T(4,128)(2,1)} reshape(bf16[32,8,16,512]{3,2,1,0:T(8,128)(2,1)} %bitcast.78) | data formatting | bytes 8388608 | tf_op jit(solution)/shard_map/while/body/eval_jaxpr/reshape | solution.py:42
  30.0 7.0 %reshape.224 = bf16[32,128,4,128]{3,2,1,0:T(4,128)(2,1)} reshape(bf16[32,8,16,512]{3,2,1,0:T(8,128)(2,1)} %bitcast.80) | data formatting | bytes 8388608 | tf_op jit(solution)/shard_map/while/body/eval_jaxpr/reshape | solution.py:41
  37.1 0.8 copy-done.5
  37.9 156.2 %while.20 = (s32[]{:T(128)}, bf16[32,4096]{1,0:T(8,128)(2,1)S(1)}, bf16[32,4096]{1,0:T(8,128)(2,1)S(1)}, pred[]{:T(512)}, bf16[32,4096]{1,0:T(8,128)(2,1)S(1)}, ...) while((s32[]{:T(128)}, bf16[32,4096]{1,0:T(8,128)(2,1)S(1)}, ...), condition=%wide.wide.region_4.5_spmd.clone, body=%wide.wide.region_0.4_spmd.clone.sunk | while | flops 71057416 | bytes 19308916 | solution.py:114
  39.1 4.6 %fusion.49 = (f32[32,4,8]{2,1,0:T(4,128)S(1)}, f32[32,4,8,128]{3,2,1,0:T(8,128)S(1)}) fusion(bf16[32,128,4,128]{3,2,1,0:T(4,128)(2,1)} %get-tuple-element.615, f32[32,4,8,128]{3,2,1,0:T(8,128)S(1)} %bitcast.76, f32[4,8,128]{2,1,0:T(8,128)S(1)} %bitcast_convert_fusion.3, f32[32,4,8]{2,1,0:T(4,128)S(1)} %copy.58, ...), kind=kOutput, calls=%fused_computation.55.clone.clone.1 | convolution fusion | flops 34339840 | bytes 5271552 | tf_op jit(solution)/shard_map/while/body/eval_jaxpr/rkgd,rtkd->rkgt/dot_general | solution.py:47
  44.3 3.4 %fusion.53 = f32[32,4,8,128]{3,2,1,0:T(8,128)S(1)} fusion(bf16[32,128,4,128]{3,2,1,0:T(4,128)(2,1)} %get-tuple-element.614, f32[32,4,8,128]{3,2,1,0:T(8,128)S(1)} %get-tuple-element.562, f32[32,4,128]{2,1,0:T(4,128)S(1)} %reshape.231, f32[32,4,8]{2,1,0:T(4,128)S(1)} %get-tuple-element.564, f32[32,4,8]{2,1,0:T(4,128)S(1)} %get-tuple-element.565, ...), kind=kOutput, calls=%fused_computation.11.clone.clone.1 | convolution fusion | flops 34340864 | bytes 5324800 | tf_op jit(solution)/shard_map/while/body/eval_jaxpr/rkgt,rtkd->rkgd/dot_general | solution.py:61
  48.1 3.4 %collective-permute-start = (bf16[32,4096]{1,0:T(8,128)(2,1)S(1)}, bf16[32,4096]{1,0:T(8,128)(2,1)S(1)}, u32[]{:S(2)}, u32[]{:S(2)}) collective-permute-start(bf16[32,4096]{1,0:T(8,128)(2,1)S(1)} %get-tuple-element.566), channel_id=1, source_target_pairs={{0,2},{2,4},{4,6},{6,8},{8,10},{10,12},{12,14},{1,3},{3,5},{5,7},{... | collective-permute-start | bytes 786440 | tf_op jit(solution)/shard_map/while/body/eval_jaxpr/ppermute | solution.py:21
  51.6 6.8 %collective-permute-done = bf16[32,4096]{1,0:T(8,128)(2,1)S(1)} collective-permute-done((bf16[32,4096]{1,0:T(8,128)(2,1)S(1)}, bf16[32,4096]{1,0:T(8,128)(2,1)S(1)}, u32[]{:S(2)}, u32[]{:S(2)}) %collective-permute-start) | collective-permute-done | bytes 262176 | tf_op jit(solution)/shard_map/while/body/eval_jaxpr/ppermute | solution.py:21
  59.6 4.6 %fusion.49 = (f32[32,4,8]{2,1,0:T(4,128)S(1)}, f32[32,4,8,128]{3,2,1,0:T(8,128)S(1)}) fusion(bf16[32,128,4,128]{3,2,1,0:T(4,128)(2,1)} %get-tuple-element.615, f32[32,4,8,128]{3,2,1,0:T(8,128)S(1)} %bitcast.76, f32[4,8,128]{2,1,0:T(8,128)S(1)} %bitcast_convert_fusion.3, f32[32,4,8]{2,1,0:T(4,128)S(1)} %copy.58, ...), kind=kOutput, calls=%fused_computation.55.clone.clone.1 | convolution fusion | flops 34339840 | bytes 5271552 | tf_op jit(solution)/shard_map/while/body/eval_jaxpr/rkgd,rtkd->rkgt/dot_general | solution.py:47
  64.8 3.4 %fusion.53 = f32[32,4,8,128]{3,2,1,0:T(8,128)S(1)} fusion(bf16[32,128,4,128]{3,2,1,0:T(4,128)(2,1)} %get-tuple-element.614, f32[32,4,8,128]{3,2,1,0:T(8,128)S(1)} %get-tuple-element.562, f32[32,4,128]{2,1,0:T(4,128)S(1)} %reshape.231, f32[32,4,8]{2,1,0:T(4,128)S(1)} %get-tuple-element.564, f32[32,4,8]{2,1,0:T(4,128)S(1)} %get-tuple-element.565, ...), kind=kOutput, calls=%fused_computation.11.clone.clone.1 | convolution fusion | flops 34340864 | bytes 5324800 | tf_op jit(solution)/shard_map/while/body/eval_jaxpr/rkgt,rtkd->rkgd/dot_general | solution.py:61
  68.6 2.5 %collective-permute-start = (bf16[32,4096]{1,0:T(8,128)(2,1)S(1)}, bf16[32,4096]{1,0:T(8,128)(2,1)S(1)}, u32[]{:S(2)}, u32[]{:S(2)}) collective-permute-start(bf16[32,4096]{1,0:T(8,128)(2,1)S(1)} %get-tuple-element.566), channel_id=1, source_target_pairs={{0,2},{2,4},{4,6},{6,8},{8,10},{10,12},{12,14},{1,3},{3,5},{5,7},{... | collective-permute-start | bytes 786440 | tf_op jit(solution)/shard_map/while/body/eval_jaxpr/ppermute | solution.py:21
  71.2 6.8 %collective-permute-done = bf16[32,4096]{1,0:T(8,128)(2,1)S(1)} collective-permute-done((bf16[32,4096]{1,0:T(8,128)(2,1)S(1)}, bf16[32,4096]{1,0:T(8,128)(2,1)S(1)}, u32[]{:S(2)}, u32[]{:S(2)}) %collective-permute-start) | collective-permute-done | bytes 262176 | tf_op jit(solution)/shard_map/while/body/eval_jaxpr/ppermute | solution.py:21
  79.2 4.6 %fusion.49 = (f32[32,4,8]{2,1,0:T(4,128)S(1)}, f32[32,4,8,128]{3,2,1,0:T(8,128)S(1)}) fusion(bf16[32,128,4,128]{3,2,1,0:T(4,128)(2,1)} %get-tuple-element.615, f32[32,4,8,128]{3,2,1,0:T(8,128)S(1)} %bitcast.76, f32[4,8,128]{2,1,0:T(8,128)S(1)} %bitcast_convert_fusion.3, f32[32,4,8]{2,1,0:T(4,128)S(1)} %copy.58, ...), kind=kOutput, calls=%fused_computation.55.clone.clone.1 | convolution fusion | flops 34339840 | bytes 5271552 | tf_op jit(solution)/shard_map/while/body/eval_jaxpr/rkgd,rtkd->rkgt/dot_general | solution.py:47
  84.3 3.4 %fusion.53 = f32[32,4,8,128]{3,2,1,0:T(8,128)S(1)} fusion(bf16[32,128,4,128]{3,2,1,0:T(4,128)(2,1)} %get-tuple-element.614, f32[32,4,8,128]{3,2,1,0:T(8,128)S(1)} %get-tuple-element.562, f32[32,4,128]{2,1,0:T(4,128)S(1)} %reshape.231, f32[32,4,8]{2,1,0:T(4,128)S(1)} %get-tuple-element.564, f32[32,4,8]{2,1,0:T(4,128)S(1)} %get-tuple-element.565, ...), kind=kOutput, calls=%fused_computation.11.clone.clone.1 | convolution fusion | flops 34340864 | bytes 5324800 | tf_op jit(solution)/shard_map/while/body/eval_jaxpr/rkgt,rtkd->rkgd/dot_general | solution.py:61
  88.2 1.9 collective-permute-start
  90.1 7.2 %collective-permute-done = bf16[32,4096]{1,0:T(8,128)(2,1)S(1)} collective-permute-done((bf16[32,4096]{1,0:T(8,128)(2,1)S(1)}, bf16[32,4096]{1,0:T(8,128)(2,1)S(1)}, u32[]{:S(2)}, u32[]{:S(2)}) %collective-permute-start) | collective-permute-done | bytes 262176 | tf_op jit(solution)/shard_map/while/body/eval_jaxpr/ppermute | solution.py:21
  98.5 4.6 %fusion.49 = (f32[32,4,8]{2,1,0:T(4,128)S(1)}, f32[32,4,8,128]{3,2,1,0:T(8,128)S(1)}) fusion(bf16[32,128,4,128]{3,2,1,0:T(4,128)(2,1)} %get-tuple-element.615, f32[32,4,8,128]{3,2,1,0:T(8,128)S(1)} %bitcast.76, f32[4,8,128]{2,1,0:T(8,128)S(1)} %bitcast_convert_fusion.3, f32[32,4,8]{2,1,0:T(4,128)S(1)} %copy.58, ...), kind=kOutput, calls=%fused_computation.55.clone.clone.1 | convolution fusion | flops 34339840 | bytes 5271552 | tf_op jit(solution)/shard_map/while/body/eval_jaxpr/rkgd,rtkd->rkgt/dot_general | solution.py:47
  103.7 3.4 %fusion.53 = f32[32,4,8,128]{3,2,1,0:T(8,128)S(1)} fusion(bf16[32,128,4,128]{3,2,1,0:T(4,128)(2,1)} %get-tuple-element.614, f32[32,4,8,128]{3,2,1,0:T(8,128)S(1)} %get-tuple-element.562, f32[32,4,128]{2,1,0:T(4,128)S(1)} %reshape.231, f32[32,4,8]{2,1,0:T(4,128)S(1)} %get-tuple-element.564, f32[32,4,8]{2,1,0:T(4,128)S(1)} %get-tuple-element.565, ...), kind=kOutput, calls=%fused_computation.11.clone.clone.1 | convolution fusion | flops 34340864 | bytes 5324800 | tf_op jit(solution)/shard_map/while/body/eval_jaxpr/rkgt,rtkd->rkgd/dot_general | solution.py:61
  107.5 1.9 collective-permute-start
  109.5 7.2 %collective-permute-done = bf16[32,4096]{1,0:T(8,128)(2,1)S(1)} collective-permute-done((bf16[32,4096]{1,0:T(8,128)(2,1)S(1)}, bf16[32,4096]{1,0:T(8,128)(2,1)S(1)}, u32[]{:S(2)}, u32[]{:S(2)}) %collective-permute-start) | collective-permute-done | bytes 262176 | tf_op jit(solution)/shard_map/while/body/eval_jaxpr/ppermute | solution.py:21
  117.9 4.6 %fusion.49 = (f32[32,4,8]{2,1,0:T(4,128)S(1)}, f32[32,4,8,128]{3,2,1,0:T(8,128)S(1)}) fusion(bf16[32,128,4,128]{3,2,1,0:T(4,128)(2,1)} %get-tuple-element.615, f32[32,4,8,128]{3,2,1,0:T(8,128)S(1)} %bitcast.76, f32[4,8,128]{2,1,0:T(8,128)S(1)} %bitcast_convert_fusion.3, f32[32,4,8]{2,1,0:T(4,128)S(1)} %copy.58, ...), kind=kOutput, calls=%fused_computation.55.clone.clone.1 | convolution fusion | flops 34339840 | bytes 5271552 | tf_op jit(solution)/shard_map/while/body/eval_jaxpr/rkgd,rtkd->rkgt/dot_general | solution.py:47
  123.1 3.4 %fusion.53 = f32[32,4,8,128]{3,2,1,0:T(8,128)S(1)} fusion(bf16[32,128,4,128]{3,2,1,0:T(4,128)(2,1)} %get-tuple-element.614, f32[32,4,8,128]{3,2,1,0:T(8,128)S(1)} %get-tuple-element.562, f32[32,4,128]{2,1,0:T(4,128)S(1)} %reshape.231, f32[32,4,8]{2,1,0:T(4,128)S(1)} %get-tuple-element.564, f32[32,4,8]{2,1,0:T(4,128)S(1)} %get-tuple-element.565, ...), kind=kOutput, calls=%fused_computation.11.clone.clone.1 | convolution fusion | flops 34340864 | bytes 5324800 | tf_op jit(solution)/shard_map/while/body/eval_jaxpr/rkgt,rtkd->rkgd/dot_general | solution.py:61
  126.9 1.9 collective-permute-start
  128.8 7.2 %collective-permute-done = bf16[32,4096]{1,0:T(8,128)(2,1)S(1)} collective-permute-done((bf16[32,4096]{1,0:T(8,128)(2,1)S(1)}, bf16[32,4096]{1,0:T(8,128)(2,1)S(1)}, u32[]{:S(2)}, u32[]{:S(2)}) %collective-permute-start) | collective-permute-done | bytes 262176 | tf_op jit(solution)/shard_map/while/body/eval_jaxpr/ppermute | solution.py:21
  137.2 4.6 %fusion.49 = (f32[32,4,8]{2,1,0:T(4,128)S(1)}, f32[32,4,8,128]{3,2,1,0:T(8,128)S(1)}) fusion(bf16[32,128,4,128]{3,2,1,0:T(4,128)(2,1)} %get-tuple-element.615, f32[32,4,8,128]{3,2,1,0:T(8,128)S(1)} %bitcast.76, f32[4,8,128]{2,1,0:T(8,128)S(1)} %bitcast_convert_fusion.3, f32[32,4,8]{2,1,0:T(4,128)S(1)} %copy.58, ...), kind=kOutput, calls=%fused_computation.55.clone.clone.1 | convolution fusion | flops 34339840 | bytes 5271552 | tf_op jit(solution)/shard_map/while/body/eval_jaxpr/rkgd,rtkd->rkgt/dot_general | solution.py:47
  142.4 3.4 %fusion.53 = f32[32,4,8,128]{3,2,1,0:T(8,128)S(1)} fusion(bf16[32,128,4,128]{3,2,1,0:T(4,128)(2,1)} %get-tuple-element.614, f32[32,4,8,128]{3,2,1,0:T(8,128)S(1)} %get-tuple-element.562, f32[32,4,128]{2,1,0:T(4,128)S(1)} %reshape.231, f32[32,4,8]{2,1,0:T(4,128)S(1)} %get-tuple-element.564, f32[32,4,8]{2,1,0:T(4,128)S(1)} %get-tuple-element.565, ...), kind=kOutput, calls=%fused_computation.11.clone.clone.1 | convolution fusion | flops 34340864 | bytes 5324800 | tf_op jit(solution)/shard_map/while/body/eval_jaxpr/rkgt,rtkd->rkgd/dot_general | solution.py:61
  146.2 1.9 collective-permute-start
  148.2 7.2 %collective-permute-done = bf16[32,4096]{1,0:T(8,128)(2,1)S(1)} collective-permute-done((bf16[32,4096]{1,0:T(8,128)(2,1)S(1)}, bf16[32,4096]{1,0:T(8,128)(2,1)S(1)}, u32[]{:S(2)}, u32[]{:S(2)}) %collective-permute-start) | collective-permute-done | bytes 262176 | tf_op jit(solution)/shard_map/while/body/eval_jaxpr/ppermute | solution.py:21
  156.6 4.6 %fusion.49 = (f32[32,4,8]{2,1,0:T(4,128)S(1)}, f32[32,4,8,128]{3,2,1,0:T(8,128)S(1)}) fusion(bf16[32,128,4,128]{3,2,1,0:T(4,128)(2,1)} %get-tuple-element.615, f32[32,4,8,128]{3,2,1,0:T(8,128)S(1)} %bitcast.76, f32[4,8,128]{2,1,0:T(8,128)S(1)} %bitcast_convert_fusion.3, f32[32,4,8]{2,1,0:T(4,128)S(1)} %copy.58, ...), kind=kOutput, calls=%fused_computation.55.clone.clone.1 | convolution fusion | flops 34339840 | bytes 5271552 | tf_op jit(solution)/shard_map/while/body/eval_jaxpr/rkgd,rtkd->rkgt/dot_general | solution.py:47
  161.8 3.4 %fusion.53 = f32[32,4,8,128]{3,2,1,0:T(8,128)S(1)} fusion(bf16[32,128,4,128]{3,2,1,0:T(4,128)(2,1)} %get-tuple-element.614, f32[32,4,8,128]{3,2,1,0:T(8,128)S(1)} %get-tuple-element.562, f32[32,4,128]{2,1,0:T(4,128)S(1)} %reshape.231, f32[32,4,8]{2,1,0:T(4,128)S(1)} %get-tuple-element.564, f32[32,4,8]{2,1,0:T(4,128)S(1)} %get-tuple-element.565, ...), kind=kOutput, calls=%fused_computation.11.clone.clone.1 | convolution fusion | flops 34340864 | bytes 5324800 | tf_op jit(solution)/shard_map/while/body/eval_jaxpr/rkgt,rtkd->rkgd/dot_general | solution.py:61
  165.6 1.9 collective-permute-start
  167.5 7.2 %collective-permute-done = bf16[32,4096]{1,0:T(8,128)(2,1)S(1)} collective-permute-done((bf16[32,4096]{1,0:T(8,128)(2,1)S(1)}, bf16[32,4096]{1,0:T(8,128)(2,1)S(1)}, u32[]{:S(2)}, u32[]{:S(2)}) %collective-permute-start) | collective-permute-done | bytes 262176 | tf_op jit(solution)/shard_map/while/body/eval_jaxpr/ppermute | solution.py:21
  176.0 4.6 %fusion.49 = (f32[32,4,8]{2,1,0:T(4,128)S(1)}, f32[32,4,8,128]{3,2,1,0:T(8,128)S(1)}) fusion(bf16[32,128,4,128]{3,2,1,0:T(4,128)(2,1)} %get-tuple-element.615, f32[32,4,8,128]{3,2,1,0:T(8,128)S(1)} %bitcast.76, f32[4,8,128]{2,1,0:T(8,128)S(1)} %bitcast_convert_fusion.3, f32[32,4,8]{2,1,0:T(4,128)S(1)} %copy.58, ...), kind=kOutput, calls=%fused_computation.55.clone.clone.1 | convolution fusion | flops 34339840 | bytes 5271552 | tf_op jit(solution)/shard_map/while/body/eval_jaxpr/rkgd,rtkd->rkgt/dot_general | solution.py:47
  181.1 3.4 %fusion.53 = f32[32,4,8,128]{3,2,1,0:T(8,128)S(1)} fusion(bf16[32,128,4,128]{3,2,1,0:T(4,128)(2,1)} %get-tuple-element.614, f32[32,4,8,128]{3,2,1,0:T(8,128)S(1)} %get-tuple-element.562, f32[32,4,128]{2,1,0:T(4,128)S(1)} %reshape.231, f32[32,4,8]{2,1,0:T(4,128)S(1)} %get-tuple-element.564, f32[32,4,8]{2,1,0:T(4,128)S(1)} %get-tuple-element.565, ...), kind=kOutput, calls=%fused_computation.11.clone.clone.1 | convolution fusion | flops 34340864 | bytes 5324800 | tf_op jit(solution)/shard_map/while/body/eval_jaxpr/rkgt,rtkd->rkgd/dot_general | solution.py:61
  185.0 1.9 collective-permute-start
  186.9 7.2 %collective-permute-done = bf16[32,4096]{1,0:T(8,128)(2,1)S(1)} collective-permute-done((bf16[32,4096]{1,0:T(8,128)(2,1)S(1)}, bf16[32,4096]{1,0:T(8,128)(2,1)S(1)}, u32[]{:S(2)}, u32[]{:S(2)}) %collective-permute-start) | collective-permute-done | bytes 262176 | tf_op jit(solution)/shard_map/while/body/eval_jaxpr/ppermute | solution.py:21
  194.1 0.8 copy.70
  195.0 0.8 copy.71
  (167 shorter events, 16.8 us)
Async XLA Ops:
  0.6 12.3 %copy-start = (s32[32,8]{0,1:T(8,128)S(1)}, s32[32,8]{0,1:T(8,128)}, u32[]{:S(2)}) copy-start(s32[32,8]{0,1:T(8,128)} %param.18) | copy-start | bytes 3076
  9.8 27.2 %collective-permute-start.1 = (bf16[32,16,512]{2,1,0:T(8,128)(2,1)S(1)}, bf16[32,16,512]{2,1,0:T(8,128)(2,1)S(1)}, u32[]{:S(2)}, u32[]{:S(2)}) collective-permute-start(bf16[32,16,512]{2,1,0:T(8,128)(2,1)S(1)} %get-tuple-element.411), channel_id=1, source_target_pairs={{0,2},{2,4},{4,6},{6,8},{8,10},{10,12},{12,14},{14,0},{1,3},{3,5},... | collective-permute-start | bytes 1572872 | tf_op jit(solution)/shard_map/ppermute | solution.py:15
  11.4 25.6 %collective-permute-start.2 = (bf16[32,16,512]{2,1,0:T(8,128)(2,1)S(1)}, bf16[32,16,512]{2,1,0:T(8,128)(2,1)S(1)}, u32[]{:S(2)}, u32[]{:S(2)}) collective-permute-start(bf16[32,16,512]{2,1,0:T(8,128)(2,1)S(1)} %get-tuple-element.410), channel_id=1, source_target_pairs={{0,2},{2,4},{4,6},{6,8},{8,10},{10,12},{12,14},{14,0},{1,3},{3,5},... | collective-permute-start | bytes 1572872 | tf_op jit(solution)/shard_map/ppermute | solution.py:15
  30.0 7.0 %copy-start.8 = (bf16[1,4096]{1,0:T(2,128)(2,1)S(1)}, bf16[1,4096]{1,0:T(2,128)(2,1)}, u32[]{:S(2)}) copy-start(bf16[1,4096]{1,0:T(2,128)(2,1)} %param.17) | copy-start | bytes 24580
  30.0 7.9 %copy-start.1 = (bf16[32,4096]{1,0:T(8,128)(2,1)S(1)}, bf16[32,4096]{1,0:T(8,128)(2,1)}, u32[]{:S(2)}) copy-start(bf16[32,4096]{1,0:T(8,128)(2,1)} %param.12) | copy-start | bytes 786436
  30.0 7.9 %copy-start.3 = (bf16[1,32,512]{2,1,0:T(8,128)(2,1)S(1)}, bf16[1,32,512]{2,1,0:T(8,128)(2,1)}, u32[]{:S(2)}) copy-start(bf16[1,32,512]{2,1,0:T(8,128)(2,1)} %param.15) | copy-start | bytes 98308
  30.0 7.9 %copy-start.4 = (bf16[1,32,512]{2,1,0:T(8,128)(2,1)S(1)}, bf16[1,32,512]{2,1,0:T(8,128)(2,1)}, u32[]{:S(2)}) copy-start(bf16[1,32,512]{2,1,0:T(8,128)(2,1)} %param.16) | copy-start | bytes 98308
  30.0 7.9 %copy-start.7 = (s32[32]{0:T(128)S(1)}, s32[32]{0:T(128)}, u32[]{:S(2)}) copy-start(s32[32]{0:T(128)} %param.19) | copy-start | bytes 388
  37.0 0.8 copy-start.5
  37.9 157.1 %copy-start.6 = (bf16[32,16,512]{2,1,0:T(8,128)(2,1)S(1)}, bf16[32,16,512]{2,1,0:T(8,128)(2,1)}, u32[]{:S(2)}) copy-start(bf16[32,16,512]{2,1,0:T(8,128)(2,1)} %copy-done.5) | copy-start | bytes 1572868
  48.1 10.3 %collective-permute-start = (bf16[32,4096]{1,0:T(8,128)(2,1)S(1)}, bf16[32,4096]{1,0:T(8,128)(2,1)S(1)}, u32[]{:S(2)}, u32[]{:S(2)}) collective-permute-start(bf16[32,4096]{1,0:T(8,128)(2,1)S(1)} %get-tuple-element.566), channel_id=1, source_target_pairs={{0,2},{2,4},{4,6},{6,8},{8,10},{10,12},{12,14},{1,3},{3,5},{5,7},{... | collective-permute-start | bytes 786440 | tf_op jit(solution)/shard_map/while/body/eval_jaxpr/ppermute | solution.py:21
  68.6 9.4 %collective-permute-start = (bf16[32,4096]{1,0:T(8,128)(2,1)S(1)}, bf16[32,4096]{1,0:T(8,128)(2,1)S(1)}, u32[]{:S(2)}, u32[]{:S(2)}) collective-permute-start(bf16[32,4096]{1,0:T(8,128)(2,1)S(1)} %get-tuple-element.566), channel_id=1, source_target_pairs={{0,2},{2,4},{4,6},{6,8},{8,10},{10,12},{12,14},{1,3},{3,5},{5,7},{... | collective-permute-start | bytes 786440 | tf_op jit(solution)/shard_map/while/body/eval_jaxpr/ppermute | solution.py:21
  88.2 9.2 %collective-permute-start = (bf16[32,4096]{1,0:T(8,128)(2,1)S(1)}, bf16[32,4096]{1,0:T(8,128)(2,1)S(1)}, u32[]{:S(2)}, u32[]{:S(2)}) collective-permute-start(bf16[32,4096]{1,0:T(8,128)(2,1)S(1)} %get-tuple-element.566), channel_id=1, source_target_pairs={{0,2},{2,4},{4,6},{6,8},{8,10},{10,12},{12,14},{1,3},{3,5},{5,7},{... | collective-permute-start | bytes 786440 | tf_op jit(solution)/shard_map/while/body/eval_jaxpr/ppermute | solution.py:21
  107.5 9.2 %collective-permute-start = (bf16[32,4096]{1,0:T(8,128)(2,1)S(1)}, bf16[32,4096]{1,0:T(8,128)(2,1)S(1)}, u32[]{:S(2)}, u32[]{:S(2)}) collective-permute-start(bf16[32,4096]{1,0:T(8,128)(2,1)S(1)} %get-tuple-element.566), channel_id=1, source_target_pairs={{0,2},{2,4},{4,6},{6,8},{8,10},{10,12},{12,14},{1,3},{3,5},{5,7},{... | collective-permute-start | bytes 786440 | tf_op jit(solution)/shard_map/while/body/eval_jaxpr/ppermute | solution.py:21
  126.9 9.2 %collective-permute-start = (bf16[32,4096]{1,0:T(8,128)(2,1)S(1)}, bf16[32,4096]{1,0:T(8,128)(2,1)S(1)}, u32[]{:S(2)}, u32[]{:S(2)}) collective-permute-start(bf16[32,4096]{1,0:T(8,128)(2,1)S(1)} %get-tuple-element.566), channel_id=1, source_target_pairs={{0,2},{2,4},{4,6},{6,8},{8,10},{10,12},{12,14},{1,3},{3,5},{5,7},{... | collective-permute-start | bytes 786440 | tf_op jit(solution)/shard_map/while/body/eval_jaxpr/ppermute | solution.py:21
  146.2 9.2 %collective-permute-start = (bf16[32,4096]{1,0:T(8,128)(2,1)S(1)}, bf16[32,4096]{1,0:T(8,128)(2,1)S(1)}, u32[]{:S(2)}, u32[]{:S(2)}) collective-permute-start(bf16[32,4096]{1,0:T(8,128)(2,1)S(1)} %get-tuple-element.566), channel_id=1, source_target_pairs={{0,2},{2,4},{4,6},{6,8},{8,10},{10,12},{12,14},{1,3},{3,5},{5,7},{... | collective-permute-start | bytes 786440 | tf_op jit(solution)/shard_map/while/body/eval_jaxpr/ppermute | solution.py:21
  165.6 9.2 %collective-permute-start = (bf16[32,4096]{1,0:T(8,128)(2,1)S(1)}, bf16[32,4096]{1,0:T(8,128)(2,1)S(1)}, u32[]{:S(2)}, u32[]{:S(2)}) collective-permute-start(bf16[32,4096]{1,0:T(8,128)(2,1)S(1)} %get-tuple-element.566), channel_id=1, source_target_pairs={{0,2},{2,4},{4,6},{6,8},{8,10},{10,12},{12,14},{1,3},{3,5},{5,7},{... | collective-permute-start | bytes 786440 | tf_op jit(solution)/shard_map/while/body/eval_jaxpr/ppermute | solution.py:21
  185.0 9.2 %collective-permute-start = (bf16[32,4096]{1,0:T(8,128)(2,1)S(1)}, bf16[32,4096]{1,0:T(8,128)(2,1)S(1)}, u32[]{:S(2)}, u32[]{:S(2)}) collective-permute-start(bf16[32,4096]{1,0:T(8,128)(2,1)S(1)} %get-tuple-element.566), channel_id=1, source_target_pairs={{0,2},{2,4},{4,6},{6,8},{8,10},{10,12},{12,14},{1,3},{3,5},{5,7},{... | collective-permute-start | bytes 786440 | tf_op jit(solution)/shard_map/while/body/eval_jaxpr/ppermute | solution.py:21
  194.1 1.6 copy-start.2
where the time goes:
time: 197 us; the launch traced here: 196 us
  matrix products  67.1 us (34%)
  waiting for transfers between devices  57.1 us (29%)
  local copies, waits for them, and re-layouts  36.6 us (19%)
  starting transfers between devices  20.6 us (10%)
  other arithmetic  12.6 us (6%)
    ppermute x8, waiting for transfers between devices, from_behind_2(): lax.ppermute(value, axis, [(source, source + steps) for source in range(l...  57.1 us
    dot_general x8, matrix products, section_attention(): jnp.einsum('rkgd,rtkd->rkgt', query, keys, preferred_element_type=jnp.flo...  36.8 us
    dot_general x8, matrix products, section_attention(): jnp.einsum('rkgt,rtkd->rkgd', weights, values, preferred_element_type=jnp...  27.6 us
    ppermute x8, starting transfers between devices, from_behind_2(): lax.ppermute(value, axis, [(source, source + steps) for source in range(l...  17.5 us
    reshape x1, local copies, waits for them, and re-layouts, section_attention(): keys = keys_pool[table_rows].reshape(rows, context, kv_here, HEAD_DIM)  6.95 us
    reshape x1, local copies, waits for them, and re-layouts, section_attention(): values = values_pool[table_rows].reshape(rows, context, kv_here, HEAD_DIM)  6.93 us
    gather x2, local copies, waits for them, and re-layouts, completed_pages(): picked = pool[page_ids]  5.54 us
    gather x1, local copies, waits for them, and re-layouts, section_attention(): values = values_pool[table_rows].reshape(rows, context, kv_here, HEAD_DIM)  5 us
  transfers between devices with their start and end apart: 10, of which 8 were waited for; matrix products, arithmetic and copies ran while one was open for 12% of the time, Pallas kernels for 0%

commit v1 on v0

v1 whole, which is shorter than its diff:
```python
import functools

import jax
import jax.numpy as jnp
from jax import lax
from jax.experimental import pallas as pl
from jax.experimental.pallas import tpu as pltpu
from jax.sharding import PartitionSpec as P

HEAD_DIM = 128
PAGE = 16
EPSILON = 1e-06
SCALE = HEAD_DIM ** (-0.5)
CHUNK = 8


def relay_kernel(
    sections,
    x_ref, k_ref, v_ref, nk_ref, nv_ref, gain_ref, table_ref, length_ref,
    out_ref, rk_ref, rv_ref,
    k_pool, v_pool, x_in, stage_k, stage_v, pool_sem, recv_sem, send_sem, rep_send, rep_recv,
):
    rows, heads, _ = x_in.shape
    kv = k_pool.shape[2] // HEAD_DIM
    share = heads // kv
    pages = table_ref.shape[1]
    context = pages * PAGE
    chunks = rows // CHUNK
    me = lax.axis_index("segment")
    right = lax.rem(me + 1, sections)
    left = lax.rem(me + sections - 1, sections)

    load_k = pltpu.make_async_copy(k_ref, k_pool, pool_sem.at[0])
    load_v = pltpu.make_async_copy(v_ref, v_pool, pool_sem.at[1])
    load_k.start()
    load_v.start()

    barrier = pltpu.get_barrier_semaphore()
    for neighbour in (left, right):
        pl.semaphore_signal(
            barrier, inc=1, device_id={"segment": neighbour}, device_id_type=pl.DeviceIdType.MESH
        )
    pl.semaphore_wait(barrier, 2)

    def rows_of(c):
        return pl.ds(c * CHUNK, CHUNK)

    @pl.when(me == 0)
    def _():
        for c in range(chunks):
            pltpu.make_async_copy(
                x_ref.at[rows_of(c)], x_in.at[rows_of(c)], recv_sem.at[c]
            ).start()

    def send_of(c):
        return pltpu.make_async_remote_copy(
            src_ref=out_ref.at[rows_of(c)],
            dst_ref=x_in.at[rows_of(c)],
            send_sem=send_sem.at[c],
            recv_sem=recv_sem.at[c],
            device_id={"segment": right},
            device_id_type=pl.DeviceIdType.MESH,
        )

    replica_k = pltpu.make_async_remote_copy(
        src_ref=stage_k, dst_ref=rk_ref, send_sem=rep_send.at[0], recv_sem=rep_recv.at[0],
        device_id={"segment": right}, device_id_type=pl.DeviceIdType.MESH,
    )
    replica_v = pltpu.make_async_remote_copy(
        src_ref=stage_v, dst_ref=rv_ref, send_sem=rep_send.at[1], recv_sem=rep_recv.at[1],
        device_id={"segment": right}, device_id_type=pl.DeviceIdType.MESH,
    )

    def fill(stage, pool):
        def one(r, carry):
            length = length_ref[r]
            last = jnp.maximum(length // PAGE - 1, 0)
            page = pool[table_ref[r, last]]
            finished = jnp.full(page.shape, lax.rem(length, PAGE), jnp.int32) == 0
            stage[r] = jnp.where(finished, page, jnp.zeros_like(page))
            return carry

        lax.fori_loop(0, rows, one, 0)

    def send_replicas():
        fill(stage_k, k_pool)
        replica_k.start()
        fill(stage_v, v_pool)
        replica_v.start()

    load_k.wait()
    load_v.wait()

    @pl.when(me != 0)
    def _():
        send_replicas()

    gain = gain_ref[...].astype(jnp.float32)
    pair = 2 * share
    top = lax.broadcasted_iota(jnp.int32, (pair, HEAD_DIM), 0) < share
    token = lax.broadcasted_iota(jnp.int32, (heads, context), 1)

    def attend(c, carry):
        pltpu.make_async_copy(x_in.at[rows_of(c)], x_in.at[rows_of(c)], recv_sem.at[c]).wait()
        x = x_in[rows_of(c)].astype(jnp.float32)
        mean_square = jnp.mean(x * x, axis=-1, keepdims=True)
        query = (x * lax.rsqrt(mean_square + EPSILON) * gain[None]).astype(jnp.bfloat16)
        fresh_k = nk_ref[rows_of(c)]
        fresh_v = nv_ref[rows_of(c)]

        def spread(fresh, i):
            return jnp.concatenate(
                [
                    jnp.broadcast_to(fresh[i : i + 1, g * HEAD_DIM : (g + 1) * HEAD_DIM], (share, HEAD_DIM))
                    for g in range(kv)
                ],
                axis=0,
            )

        scores = []
        ids = []
        for i in range(CHUNK):
            r = c * CHUNK + i
            ids.append([table_ref[r, p] for p in range(pages)])
            parts = []
            for g in range(kv // 2):
                cols = slice(g * 2 * HEAD_DIM, (g + 1) * 2 * HEAD_DIM)
                keys = jnp.concatenate([k_pool[j, :, cols] for j in ids[i]], axis=0)
                q = query[i, g * pair : (g + 1) * pair]
                zero = jnp.zeros_like(q)
                wide = jnp.concatenate(
                    [jnp.where(top, q, zero), jnp.where(top, zero, q)], axis=1
                )
                parts.append(
                    lax.dot_general(
                        wide, keys, (((1,), (1,)), ((), ())), preferred_element_type=jnp.float32
                    )
                )
            s = jnp.concatenate(parts, axis=0) * SCALE
            scores.append(jnp.where(token < length_ref[r], s, -1e30))
        scores = jnp.stack(scores)
        own = jnp.stack([spread(fresh_k, i) for i in range(CHUNK)])
        own = jnp.sum(query.astype(jnp.float32) * own, axis=-1, keepdims=True) * SCALE
        highest = jnp.maximum(jnp.max(scores, axis=-1, keepdims=True), own)
        weights = jnp.exp(scores - highest)
        own = jnp.exp(own - highest)
        share_of = 1.0 / (jnp.sum(weights, axis=-1, keepdims=True) + own)
        weights = (weights * share_of).astype(jnp.bfloat16)
        own = (own * share_of).astype(jnp.bfloat16).astype(jnp.float32)
        for i in range(CHUNK):
            parts = []
            for g in range(kv // 2):
                cols = slice(g * 2 * HEAD_DIM, (g + 1) * 2 * HEAD_DIM)
                values = jnp.concatenate([v_pool[j, :, cols] for j in ids[i]], axis=0)
                mixed = jnp.dot(
                    weights[i, g * pair : (g + 1) * pair], values, preferred_element_type=jnp.float32
                )
                parts += [mixed[:share, :HEAD_DIM], mixed[share:, HEAD_DIM:]]
            result = x[i] + jnp.concatenate(parts, axis=0) + own[i] * spread(fresh_v, i)
            out_ref[c * CHUNK + i] = result.astype(jnp.bfloat16)

        @pl.when(me < sections - 1)
        def _():
            send_of(c).start()

        return carry

    lax.fori_loop(0, chunks, attend, 0)

    @pl.when(me == 0)
    def _():
        send_replicas()

    @pl.when(me < sections - 1)
    def _():
        for c in range(chunks):
            send_of(c).wait_send()

    replica_k.wait()
    replica_v.wait()


def shards(sections, stream_in, cache_k, cache_v, new_k, new_v, q_gain, page_table, lengths):
    rows, width = stream_in.shape
    heads = width // HEAD_DIM
    pool = cache_k.shape[1:]
    anywhere = pl.BlockSpec(memory_space=pl.ANY)
    vmem = pl.BlockSpec(memory_space=pltpu.VMEM)
    smem = pl.BlockSpec(memory_space=pltpu.SMEM)
    kept = (rows,) + pool[1:]
    chunks = rows // CHUNK
    out, replica_k, replica_v = pl.pallas_call(
        functools.partial(relay_kernel, sections),
        out_shape=(
            jax.ShapeDtypeStruct((rows, heads, HEAD_DIM), jnp.bfloat16),
            jax.ShapeDtypeStruct(kept, jnp.bfloat16),
            jax.ShapeDtypeStruct(kept, jnp.bfloat16),
        ),
        in_specs=[anywhere, anywhere, anywhere, vmem, vmem, vmem, smem, smem],
        out_specs=(vmem, anywhere, anywhere),
        scratch_shapes=[
            pltpu.VMEM(pool, jnp.bfloat16),
            pltpu.VMEM(pool, jnp.bfloat16),
            pltpu.VMEM((rows, heads, HEAD_DIM), jnp.bfloat16),
            pltpu.VMEM(kept, jnp.bfloat16),
            pltpu.VMEM(kept, jnp.bfloat16),
            pltpu.SemaphoreType.DMA((2,)),
            pltpu.SemaphoreType.DMA((chunks,)),
            pltpu.SemaphoreType.DMA((chunks,)),
            pltpu.SemaphoreType.DMA((2,)),
            pltpu.SemaphoreType.DMA((2,)),
        ],
        compiler_params=pltpu.CompilerParams(
            collective_id=0, has_side_effects=True, vmem_limit_bytes=40 * 1024 * 1024
        ),
        name="relay",
    )(
        stream_in.reshape(rows, heads, HEAD_DIM),
        cache_k[0],
        cache_v[0],
        new_k[0].astype(jnp.float32),
        new_v[0].astype(jnp.float32),
        q_gain.reshape(heads, HEAD_DIM),
        page_table,
        lengths,
    )
    return (out.reshape(1, rows, width), replica_k[None], replica_v[None])


def solution(mesh):
    in_specs = (
        P("group", "tensor"),
        P("segment", "group", None, "tensor"),
        P("segment", "group", None, "tensor"),
        P("segment", "group", "tensor"),
        P("segment", "group", "tensor"),
        P("segment", "tensor"),
        P("group", None),
        P("group"),
    )
    out_specs = (
        P("segment", "group", "tensor"),
        P("segment", "group", None, "tensor"),
        P("segment", "group", None, "tensor"),
    )
    return jax.shard_map(
        functools.partial(shards, mesh.shape["segment"]),
        mesh=mesh, in_specs=in_specs, out_specs=out_specs, check_vma=False,
    )
```

time: 197 us -> 65.7 us (0.33)
  the two profiles are of different devices: /device:TPU:16 before, /device:TPU:28 now
where the time goes in v1:
time: 65.7 us; the launch traced here: 65.3 us
  Pallas kernels  53.9 us (82%)
  local copies, waits for them, and re-layouts  9.18 us (14%)
  other arithmetic  1.55 us (2%)
  between operations  0.66 us (1%)
    pallas_call x1, Pallas kernels, shards(): pl.pallas_call(functools.partial(relay_kernel, sections), out_shape=(jax....  53.9 us
    unnamed x10, local copies, waits for them, and re-layouts  8.37 us

profile of v1, /device:TPU:28, one launch (start us, length us, event | category | flops | bytes accessed | tf_op | source)
XLA Modules:
  0.0 65.3 jit_solution(16689666272794323335)
XLA Ops:
  0.6 0.8 %reduce = bf16[4096]{0:T(1024)(128)(2,1)S(1)} reduce(bf16[1,4096]{1,0:T(2,128)(2,1)} %param.13, bf16[]{:T(256)} %constant.5), dimensions={0}, to_apply=%param.13.reduce_sub_computation | reduce | bytes 16386 | tf_op args[5]
  1.4 0.8 %copy.11.table_ref = s32[32,8]{1,0:T(8,128)S(1)} copy(s32[32,8]{0,1:T(8,128)} %param.14) | data formatting | bytes 2048 | tf_op args[6]
  2.2 0.8 %bitcast_convert_fusion = (f32[32,512]{1,0:T(8,128)S(1)}, f32[32,512]{1,0:T(8,128)S(1)}) fusion(bf16[1,32,512]{2,1,0:T(8,128)(2,1)} %param.12, bf16[1,32,512]{2,1,0:T(8,128)(2,1)} %param.11), kind=kLoop, calls=%fused_computation | loop fusion | flops 32768 | bytes 196608 | tf_op jit(solution)/shard_map/convert_element_type | solution.py:222
  3.0 1.0 %copy.12 = bf16[4,8,32,128]{3,2,1,0:T(8,128)(2,1)S(1)} copy(bf16[4,8,32,128]{3,1,2,0:T(8,128)(2,1)} %bitcast.19) | data formatting | bytes 524288
  4.0 0.0 copy-start
  4.0 2.2 %copy-done = bf16[1,256,16,512]{3,2,1,0:T(8,128)(2,1)S(1)} copy-done((bf16[1,256,16,512]{3,2,1,0:T(8,128)(2,1)S(1)}, bf16[1,256,16,512]{3,2,1,0:T(8,128)(2,1)}, u32[]{:S(2)}) %copy-start) | copy-done | bytes 4194328
  6.1 0.0 copy-start.1
  6.1 2.2 %copy-done.1 = bf16[1,256,16,512]{3,2,1,0:T(8,128)(2,1)S(1)} copy-done((bf16[1,256,16,512]{3,2,1,0:T(8,128)(2,1)S(1)}, bf16[1,256,16,512]{3,2,1,0:T(8,128)(2,1)}, u32[]{:S(2)}) %copy-start.1) | copy-done | bytes 4194328
  8.3 0.0 copy-start.2
  8.3 0.7 copy-done.2
  9.0 53.9 %relay.1 = (bf16[32,32,128]{2,1,0:T(8,128)(2,1)S(1)}, bf16[32,16,512]{2,1,0:T(8,128)(2,1)S(1)}, bf16[32,16,512]{2,1,0:T(8,128)(2,1)S(1)}) custom-call(bf16[32,32,128]{2,1,0:T(8,128)(2,1)S(1)} %bitcast.15, bf16[256,16,512]{2,1,0:T(8,128)(2,1)S(1)} %bitcast.13, bf16[256,16,512]{2,1,0:T(8,128)(2,1)S(1)} %bitcast.14, f32[32,512]{1,0:T(8,128)S(1)} %get-tuple-element.10.nk_ref, ...), custom_call_target="tpu_custom_call" | custom-call | tf_op jit(solution)/shard_map/relay/pallas_call | solution.py:192
  62.9 0.8 %reshape.21 = bf16[1,32,4096]{2,1,0:T(8,128)(2,1)} reshape(bf16[32,32,128]{2,1,0:T(8,128)(2,1)S(1)} %get-tuple-element.6) | data formatting | bytes 524288 | tf_op jit(solution)/shard_map/reshape | solution.py:227
  63.7 0.8 %copy.15 = bf16[1,32,16,512]{3,2,1,0:T(8,128)(2,1)} copy(bf16[1,32,16,512]{3,2,1,0:T(8,128)(2,1)S(1)} %bitcast.17) | data formatting | bytes 1048576
  64.5 0.8 %copy.16 = bf16[1,32,16,512]{3,2,1,0:T(8,128)(2,1)} copy(bf16[1,32,16,512]{3,2,1,0:T(8,128)(2,1)S(1)} %bitcast.16) | data formatting | bytes 1048576
Async XLA Ops:
  4.0 2.2 %copy-start = (bf16[1,256,16,512]{3,2,1,0:T(8,128)(2,1)S(1)}, bf16[1,256,16,512]{3,2,1,0:T(8,128)(2,1)}, u32[]{:S(2)}) copy-start(bf16[1,256,16,512]{3,2,1,0:T(8,128)(2,1)} %param.9) | copy-start | bytes 12582916
  6.1 2.2 %copy-start.1 = (bf16[1,256,16,512]{3,2,1,0:T(8,128)(2,1)S(1)}, bf16[1,256,16,512]{3,2,1,0:T(8,128)(2,1)}, u32[]{:S(2)}) copy-start(bf16[1,256,16,512]{3,2,1,0:T(8,128)(2,1)} %param.10) | copy-start | bytes 12582916
  8.3 0.7 %copy-start.2 = (s32[32]{0:T(128)S(1)}, s32[32]{0:T(128)}, u32[]{:S(2)}) copy-start(s32[32]{0:T(128)} %length_ref.1) | copy-start | bytes 388

commit v2 on v1

v2 whole, which is shorter than its diff:
```python
import functools

import jax
import jax.numpy as jnp
from jax import lax
from jax.experimental import pallas as pl
from jax.experimental.pallas import tpu as pltpu
from jax.sharding import PartitionSpec as P

HEAD_DIM = 128
PAGE = 16
EPSILON = 1e-06
SCALE = HEAD_DIM ** (-0.5)
CHUNK = 4
PIECE = 8
VMEM_BYTES = 60 * 1024 * 1024


def pieces_before(section):
    return section * 3 // 2


def relay_kernel(
    sections,
    x_hbm, k_hbm, v_hbm, nk_hbm, nv_hbm, gain_hbm, table_hbm, length_hbm,
    out_ref, replica_ref,
    k_pool, v_pool, x_raw, x_wide, x_in, stage, nk_ref, nv_ref, gain_row, gain_ref, table_ref, length_ref,
    load_sem, recv_sem, send_sem, rep_send, rep_recv,
):
    rows, heads, _ = x_in.shape
    kv = k_pool.shape[2] // HEAD_DIM
    share = heads // kv
    pages = table_ref.shape[0]
    context = pages * PAGE
    chunks = rows // CHUNK
    pieces = 2 * rows // PIECE
    me = lax.axis_index("segment")
    right = lax.rem(me + 1, sections)
    left = lax.rem(me + sections - 1, sections)

    loads = [
        pltpu.make_async_copy(source, target, load_sem.at[i])
        for i, (source, target) in enumerate(
            (
                (table_hbm, table_ref),
                (length_hbm, length_ref),
                (x_hbm, x_raw),
                (gain_hbm, gain_row),
                (nk_hbm, nk_ref),
                (nv_hbm, nv_ref),
                (k_hbm, k_pool),
                (v_hbm, v_pool),
            )
        )
    ]
    for load in loads:
        load.start()

    barrier = pltpu.get_barrier_semaphore()
    pl.semaphore_signal(
        barrier, inc=1, device_id={"segment": left}, device_id_type=pl.DeviceIdType.MESH
    )
    for load in loads[:4]:
        load.wait()

    def columns(h):
        return slice(h * HEAD_DIM, (h + 1) * HEAD_DIM)

    @pl.when(me == 0)
    def _():
        for h in range(heads):
            x_wide[:, h, :] = x_raw[:, columns(h)].astype(jnp.float32)
        x_in[...] = x_wide[...].astype(jnp.bfloat16)

    gain_wide = gain_row[...].astype(jnp.float32)
    for h in range(heads):
        gain_ref[h : h + 1, :] = gain_wide[:, columns(h)]

    for load in loads[4:]:
        load.wait()
    pl.semaphore_wait(barrier, 1)

    def rows_of(c):
        return pl.ds(c * CHUNK, CHUNK)

    def send_of(c):
        return pltpu.make_async_remote_copy(
            src_ref=out_ref.at[rows_of(c)],
            dst_ref=x_in.at[rows_of(c)],
            send_sem=send_sem.at[c],
            recv_sem=recv_sem.at[c],
            device_id={"segment": right},
            device_id_type=pl.DeviceIdType.MESH,
        )

    def piece_of(i):
        return pltpu.make_async_remote_copy(
            src_ref=stage.at[pl.ds(i * PIECE, PIECE)],
            dst_ref=replica_ref.at[pl.ds(i * PIECE, PIECE)],
            send_sem=rep_send.at[i],
            recv_sem=rep_recv.at[i],
            device_id={"segment": right},
            device_id_type=pl.DeviceIdType.MESH,
        )

    def fill():
        def one(r, carry):
            length = length_ref[r]
            last = jnp.maximum(length // PAGE - 1, 0)
            page_id = table_ref[last, r]
            for first, pool in ((0, k_pool), (rows, v_pool)):
                page = pool[page_id]
                finished = jnp.full(page.shape, lax.rem(length, PAGE), jnp.int32) == 0
                stage[first + r] = jnp.where(finished, page, jnp.zeros_like(page))
            return carry

        lax.fori_loop(0, rows, one, 0)

    def send_pieces(first, last):
        def one(i, carry):
            piece_of(i).start()
            return carry

        lax.fori_loop(first, last, one, 0)

    before = jnp.where(me == sections - 1, pieces, jnp.minimum(pieces_before(me), pieces))

    @pl.when(me != 0)
    def _():
        fill()
        send_pieces(0, before)

    gain = gain_ref[...]
    pair = 2 * share
    top = lax.broadcasted_iota(jnp.int32, (pair, HEAD_DIM), 0) < share
    token = lax.broadcasted_iota(jnp.int32, (heads, context), 1)

    def attend(c, fresh_k, fresh_v):
        @pl.when(me > 0)
        def _():
            send_of(c).wait_recv()

        x = x_in[rows_of(c)].astype(jnp.float32)
        mean_square = jnp.mean(x * x, axis=-1, keepdims=True)
        query = (x * lax.rsqrt(mean_square + EPSILON) * gain[None]).astype(jnp.bfloat16)

        def spread(fresh, i):
            return jnp.concatenate(
                [
                    jnp.broadcast_to(fresh[i : i + 1, columns(g)], (share, HEAD_DIM))
                    for g in range(kv)
                ],
                axis=0,
            )

        scores = []
        ids = []
        for i in range(CHUNK):
            r = c * CHUNK + i
            ids.append([table_ref[p, r] for p in range(pages)])
            parts = []
            for g in range(kv // 2):
                cols = slice(g * 2 * HEAD_DIM, (g + 1) * 2 * HEAD_DIM)
                keys = jnp.concatenate([k_pool[j, :, cols] for j in ids[i]], axis=0)
                q = query[i, g * pair : (g + 1) * pair]
                zero = jnp.zeros_like(q)
                wide = jnp.concatenate(
                    [jnp.where(top, q, zero), jnp.where(top, zero, q)], axis=1
                )
                parts.append(
                    lax.dot_general(
                        wide, keys, (((1,), (1,)), ((), ())), preferred_element_type=jnp.float32
                    )
                )
            s = jnp.concatenate(parts, axis=0) * SCALE
            scores.append(jnp.where(token < length_ref[r], s, -1e30))
        scores = jnp.stack(scores)
        own = jnp.stack([spread(fresh_k, i) for i in range(CHUNK)])
        own = jnp.sum(query.astype(jnp.float32) * own, axis=-1, keepdims=True) * SCALE
        highest = jnp.maximum(jnp.max(scores, axis=-1, keepdims=True), own)
        weights = jnp.exp(scores - highest)
        own = jnp.exp(own - highest)
        share_of = 1.0 / (jnp.sum(weights, axis=-1, keepdims=True) + own)
        weights = (weights * share_of).astype(jnp.bfloat16)
        own = (own * share_of).astype(jnp.bfloat16).astype(jnp.float32)
        for i in range(CHUNK):
            parts = []
            for g in range(kv // 2):
                cols = slice(g * 2 * HEAD_DIM, (g + 1) * 2 * HEAD_DIM)
                values = jnp.concatenate([v_pool[j, :, cols] for j in ids[i]], axis=0)
                mixed = jnp.dot(
                    weights[i, g * pair : (g + 1) * pair], values, preferred_element_type=jnp.float32
                )
                parts += [mixed[:share, :HEAD_DIM], mixed[share:, HEAD_DIM:]]
            result = x[i] + jnp.concatenate(parts, axis=0) + own[i] * spread(fresh_v, i)
            out_ref[c * CHUNK + i] = result.astype(jnp.bfloat16)

        @pl.when(me < sections - 1)
        def _():
            send_of(c).start()

    block = max(CHUNK, 16)

    def attend_block(b, carry):
        at = pl.ds(pl.multiple_of(b * block, block), block)
        fresh_k = nk_ref[at, :].astype(jnp.float32)
        fresh_v = nv_ref[at, :].astype(jnp.float32)
        for j in range(block // CHUNK):
            own = slice(j * CHUNK, (j + 1) * CHUNK)
            attend(b * (block // CHUNK) + j, fresh_k[own], fresh_v[own])
        return carry

    lax.fori_loop(0, rows // block, attend_block, 0)

    @pl.when(me == 0)
    def _():
        fill()
        send_pieces(0, before)

    send_pieces(before, pieces)

    @pl.when(me < sections - 1)
    def _():
        for c in range(chunks):
            send_of(c).wait_send()

    for i in range(pieces):
        piece_of(i).wait()


def shards(sections, stream_in, cache_k, cache_v, new_k, new_v, q_gain, page_table, lengths):
    rows, width = stream_in.shape
    heads = width // HEAD_DIM
    pool = cache_k.shape[1:]
    hbm = pl.BlockSpec(memory_space=pltpu.HBM)
    vmem = pl.BlockSpec(memory_space=pltpu.VMEM)
    chunks = rows // CHUNK
    pieces = 2 * rows // PIECE
    fresh = new_k.shape[1:]
    both = (2 * rows,) + pool[1:]
    out, replicas = pl.pallas_call(
        functools.partial(relay_kernel, sections),
        out_shape=(
            jax.ShapeDtypeStruct((rows, heads, HEAD_DIM), jnp.bfloat16),
            jax.ShapeDtypeStruct(both, jnp.bfloat16),
        ),
        in_specs=[hbm] * 8,
        out_specs=(vmem, vmem),
        scratch_shapes=[
            pltpu.VMEM(pool, jnp.bfloat16),
            pltpu.VMEM(pool, jnp.bfloat16),
            pltpu.VMEM((rows, width), jnp.bfloat16),
            pltpu.VMEM((rows, heads, HEAD_DIM), jnp.float32),
            pltpu.VMEM((rows, heads, HEAD_DIM), jnp.bfloat16),
            pltpu.VMEM(both, jnp.bfloat16),
            pltpu.VMEM(fresh, jnp.bfloat16),
            pltpu.VMEM(fresh, jnp.bfloat16),
            pltpu.VMEM((1, width), jnp.bfloat16),
            pltpu.VMEM((heads, HEAD_DIM), jnp.float32),
            pltpu.SMEM(page_table.shape[::-1], jnp.int32),
            pltpu.SMEM(lengths.shape, jnp.int32),
            pltpu.SemaphoreType.DMA((8,)),
            pltpu.SemaphoreType.DMA((chunks,)),
            pltpu.SemaphoreType.DMA((chunks,)),
            pltpu.SemaphoreType.DMA((pieces,)),
            pltpu.SemaphoreType.DMA((pieces,)),
        ],
        compiler_params=pltpu.CompilerParams(
            collective_id=0, has_side_effects=True, vmem_limit_bytes=VMEM_BYTES
        ),
        name="relay",
    )(
        stream_in,
        cache_k[0],
        cache_v[0],
        new_k[0],
        new_v[0],
        q_gain,
        page_table.T,
        lengths,
    )
    return (out.reshape(1, rows, width), replicas[None, :rows], replicas[None, rows:])


def solution(mesh):
    in_specs = (
        P("group", "tensor"),
        P("segment", "group", None, "tensor"),
        P("segment", "group", None, "tensor"),
        P("segment", "group", "tensor"),
        P("segment", "group", "tensor"),
        P("segment", "tensor"),
        P("group", None),
        P("group"),
    )
    out_specs = (
        P("segment", "group", "tensor"),
        P("segment", "group", None, "tensor"),
        P("segment", "group", None, "tensor"),
    )
    return jax.shard_map(
        functools.partial(shards, mesh.shape["segment"]),
        mesh=mesh, in_specs=in_specs, out_specs=out_specs, check_vma=False,
    )
```

time: 65.7 us -> 42.9 us (0.65)
  Pallas kernels: 53.9 us -> 38.1 us
  local copies, waits for them, and re-layouts: 9.18 us -> 4 us
  other arithmetic: 1.55 us -> 0 us
    pallas_call x1, Pallas kernels: 53.9 us -> 38.1 us  [shards(): pl.pallas_call(functools.partial(relay_kernel, sections), out_shape=(jax....]
    unnamed x10 -> x0, local copies, waits for them, and re-layouts: 8.37 us -> none
    broadcast_in_dim x0 -> x1, local copies, waits for them, and re-layouts: none -> 2.23 us  [shards(): replicas[None, rows:]]
    reshape x1, local copies, waits for them, and re-layouts: 0.82 us -> 1.77 us  [shards(): out.reshape(1, rows, width)]
    convert_element_type x1 -> x0, other arithmetic: 0.78 us -> none  [shards(): new_v[0].astype(jnp.float32)]
    unnamed x1 -> x0, other arithmetic: 0.77 us -> none
where the time goes in v2:
time: 42.9 us; the launch traced here: 42.7 us
  Pallas kernels  38.1 us (89%)
  local copies, waits for them, and re-layouts  4 us (9%)
  between operations  0.64 us (1%)
    pallas_call x1, Pallas kernels, shards(): pl.pallas_call(functools.partial(relay_kernel, sections), out_shape=(jax....  38.1 us
    broadcast_in_dim x1, local copies, waits for them, and re-layouts, shards(): replicas[None, rows:]  2.23 us
    reshape x1, local copies, waits for them, and re-layouts, shards(): out.reshape(1, rows, width)  1.77 us

profile of v2, /device:TPU:28, one launch (start us, length us, event | category | flops | bytes accessed | tf_op | source)
XLA Modules:
  0.0 42.7 jit_solution(17373065363408755235)
XLA Ops:
  0.6 38.1 %relay.1 = (bf16[32,32,128]{2,1,0:T(8,128)(2,1)}, bf16[64,16,512]{2,1,0:T(8,128)(2,1)}) custom-call(bf16[32,4096]{1,0:T(8,128)(2,1)} %x_hbm.1, bf16[256,16,512]{2,1,0:T(8,128)(2,1)} %bitcast.9, bf16[256,16,512]{2,1,0:T(8,128)(2,1)} %bitcast.10, bf16[32,512]{1,0:T(8,128)(2,1)} %bitcast.11, bf16[32,512]{1,0:T(8,128)(2,1)} %bitcast.12, ...), custom_call_target="tpu_custom_call" | custom-call | tf_op jit(solution)/shard_map/relay/pallas_call | solution.py:241
  38.7 1.8 %reshape.9 = bf16[1,32,4096]{2,1,0:T(8,128)(2,1)} reshape(bf16[32,32,128]{2,1,0:T(8,128)(2,1)} %get-tuple-element.5) | data formatting | bytes 524288 | tf_op jit(solution)/shard_map/reshape | solution.py:282
  40.5 2.2 %slice_bitcast_fusion = (bf16[1,32,16,512]{3,2,1,0:T(8,128)(2,1)}, bf16[1,32,16,512]{3,2,1,0:T(8,128)(2,1)}) fusion(bf16[64,16,512]{2,1,0:T(8,128)(2,1)} %get-tuple-element.6), kind=kLoop, calls=%fused_computation | loop fusion | bytes 2097152 | tf_op jit(solution)/shard_map/broadcast_in_dim | solution.py:282

commit v3 on v2

--- a/solution.py
+++ b/solution.py
@@ -17,7 +17,7 @@
 
 
 def pieces_before(section):
-    return section * 3 // 2
+    return section * 5 // 4
 
 
 def relay_kernel(
@@ -226,6 +226,32 @@
 
     for i in range(pieces):
         piece_of(i).wait()
+
+
+def finish_kernel(x_hbm, pages_hbm, out_hbm, rk_hbm, rv_hbm, x, wide, flat, pages, sem):
+    rows, heads, _ = x.shape
+    load_x = pltpu.make_async_copy(x_hbm, x, sem.at[0])
+    load_x.start()
+    halves = [pl.ds(0, rows), pl.ds(rows, rows)]
+    load_pages = [
+        pltpu.make_async_copy(pages_hbm.at[half], pages.at[half], sem.at[1 + i])
+        for i, half in enumerate(halves)
+    ]
+    for load in load_pages:
+        load.start()
+    load_x.wait()
+    wide[...] = x[...].astype(jnp.float32)
+    for h in range(heads):
+        flat[:, h * HEAD_DIM : (h + 1) * HEAD_DIM] = wide[:, h, :].astype(jnp.bfloat16)
+    stores = [pltpu.make_async_copy(flat, out_hbm.at[0], sem.at[3])]
+    stores[0].start()
+    for i, target in enumerate((rk_hbm, rv_hbm)):
+        load_pages[i].wait()
+        store = pltpu.make_async_copy(pages.at[halves[i]], target.at[0], sem.at[4 + i])
+        store.start()
+        stores.append(store)
+    for store in stores:
+        store.wait()
 
 
 def shards(sections, stream_in, cache_k, cache_v, new_k, new_v, q_gain, page_table, lengths):
@@ -279,7 +305,26 @@
         page_table.T,
         lengths,
     )
-    return (out.reshape(1, rows, width), replicas[None, :rows], replicas[None, rows:])
+    kept = (1, rows) + pool[1:]
+    return pl.pallas_call(
+        finish_kernel,
+        out_shape=(
+            jax.ShapeDtypeStruct((1, rows, width), jnp.bfloat16),
+            jax.ShapeDtypeStruct(kept, jnp.bfloat16),
+            jax.ShapeDtypeStruct(kept, jnp.bfloat16),
+        ),
+        in_specs=[hbm, hbm],
+        out_specs=(hbm, hbm, hbm),
+        scratch_shapes=[
+            pltpu.VMEM((rows, heads, HEAD_DIM), jnp.bfloat16),
+            pltpu.VMEM((rows, heads, HEAD_DIM), jnp.float32),
+            pltpu.VMEM((rows, width), jnp.bfloat16),
+            pltpu.VMEM(both, jnp.bfloat16),
+            pltpu.SemaphoreType.DMA((6,)),
+        ],
+        compiler_params=pltpu.CompilerParams(vmem_limit_bytes=VMEM_BYTES),
+        name="finish",
+    )(out, replicas)
 
 
 def solution(mesh):

time: 42.9 us -> 40.9 us (0.953); the launches traced: 42.7 us -> 40.1 us
  local copies, waits for them, and re-layouts: 4 us -> 0 us
  Pallas kernels: 38.1 us -> 39.5 us
    pallas_call x0 -> x1, Pallas kernels: none -> 2.61 us  [shards(): pl.pallas_call(finish_kernel, out_shape=(jax.ShapeDtypeStruct((1, rows, w...]
    broadcast_in_dim x1 -> x0, local copies, waits for them, and re-layouts: 2.23 us -> none  [shards(): replicas[None, rows:]]
    reshape x1 -> x0, local copies, waits for them, and re-layouts: 1.77 us -> none  [shards(): out.reshape(1, rows, width)]
    pallas_call x1, Pallas kernels: 38.1 us -> 36.9 us  [shards(): pl.pallas_call(functools.partial(relay_kernel, sections), out_shape=(jax....]
where the time goes in v3:
time: 40.9 us; the launch traced here: 40.1 us
  Pallas kernels  39.5 us (97%)
  between operations  0.64 us (2%)
    pallas_call x1, Pallas kernels, shards(): pl.pallas_call(functools.partial(relay_kernel, sections), out_shape=(jax....  36.9 us
    pallas_call x1, Pallas kernels, shards(): pl.pallas_call(finish_kernel, out_shape=(jax.ShapeDtypeStruct((1, rows, w...  2.61 us

profile of v3, /device:TPU:28, one launch (start us, length us, event | category | flops | bytes accessed | tf_op | source)
XLA Modules:
  0.0 40.1 jit_solution(2397665051613002289)
XLA Ops:
  0.6 36.9 %relay.1 = (bf16[32,32,128]{2,1,0:T(8,128)(2,1)}, bf16[64,16,512]{2,1,0:T(8,128)(2,1)}) custom-call(bf16[32,4096]{1,0:T(8,128)(2,1)} %x_hbm.1, bf16[256,16,512]{2,1,0:T(8,128)(2,1)} %bitcast.5, bf16[256,16,512]{2,1,0:T(8,128)(2,1)} %bitcast.6, bf16[32,512]{1,0:T(8,128)(2,1)} %bitcast.7, bf16[32,512]{1,0:T(8,128)(2,1)} %bitcast.8, bf16[1,4096]{1,0:T(2,128)(2,1)} %gain_hbm.1, ...), custom_call_target="tpu_custom_call" | custom-call | tf_op jit(solution)/shard_map/relay/pallas_call | solution.py:267
  37.5 2.6 %finish.1 = (bf16[1,32,4096]{2,1,0:T(8,128)(2,1)}, bf16[1,32,16,512]{3,2,1,0:T(8,128)(2,1)}, bf16[1,32,16,512]{3,2,1,0:T(8,128)(2,1)}) custom-call(bf16[32,32,128]{2,1,0:T(8,128)(2,1)} %get-tuple-element.5.x_hbm, bf16[64,16,512]{2,1,0:T(8,128)(2,1)} %get-tuple-element.6.pages_hbm), custom_call_target="tpu_custom_call" | custom-call | tf_op jit(solution)/shard_map/finish/pallas_call | solution.py:309

commit v4 on v3

--- a/solution.py
+++ b/solution.py
@@ -17,7 +17,7 @@
 
 
 def pieces_before(section):
-    return section * 5 // 4
+    return section * 3 // 2
 
 
 def relay_kernel(
@@ -76,7 +76,7 @@
     for h in range(heads):
         gain_ref[h : h + 1, :] = gain_wide[:, columns(h)]
 
-    for load in loads[4:]:
+    for load in loads[4:7]:
         load.wait()
     pl.semaphore_wait(barrier, 1)
 
@@ -103,18 +103,18 @@
             device_id_type=pl.DeviceIdType.MESH,
         )
 
-    def fill():
-        def one(r, carry):
-            length = length_ref[r]
-            last = jnp.maximum(length // PAGE - 1, 0)
-            page_id = table_ref[last, r]
-            for first, pool in ((0, k_pool), (rows, v_pool)):
-                page = pool[page_id]
+    def fill(first, pool):
+        def one(b, carry):
+            for j in range(4):
+                r = b * 4 + j
+                length = length_ref[r]
+                last = jnp.maximum(length // PAGE - 1, 0)
+                page = pool[table_ref[last, r]]
                 finished = jnp.full(page.shape, lax.rem(length, PAGE), jnp.int32) == 0
                 stage[first + r] = jnp.where(finished, page, jnp.zeros_like(page))
             return carry
 
-        lax.fori_loop(0, rows, one, 0)
+        lax.fori_loop(0, rows // 4, one, 0)
 
     def send_pieces(first, last):
         def one(i, carry):
@@ -125,10 +125,19 @@
 
     before = jnp.where(me == sections - 1, pieces, jnp.minimum(pieces_before(me), pieces))
 
+    half = pieces // 2
+
     @pl.when(me != 0)
     def _():
-        fill()
-        send_pieces(0, before)
+        fill(0, k_pool)
+        send_pieces(0, jnp.minimum(before, half))
+
+    loads[7].wait()
+
+    @pl.when(me != 0)
+    def _():
+        fill(rows, v_pool)
+        send_pieces(jnp.minimum(before, half), before)
 
     gain = gain_ref[...]
     pair = 2 * share
@@ -172,17 +181,17 @@
                         wide, keys, (((1,), (1,)), ((), ())), preferred_element_type=jnp.float32
                     )
                 )
-            s = jnp.concatenate(parts, axis=0) * SCALE
+            s = jnp.concatenate(parts, axis=0)
             scores.append(jnp.where(token < length_ref[r], s, -1e30))
         scores = jnp.stack(scores)
         own = jnp.stack([spread(fresh_k, i) for i in range(CHUNK)])
-        own = jnp.sum(query.astype(jnp.float32) * own, axis=-1, keepdims=True) * SCALE
+        own = jnp.sum(query.astype(jnp.float32) * own, axis=-1, keepdims=True)
         highest = jnp.maximum(jnp.max(scores, axis=-1, keepdims=True), own)
-        weights = jnp.exp(scores - highest)
-        own = jnp.exp(own - highest)
+        weights = jnp.exp((scores - highest) * SCALE)
+        own = jnp.exp((own - highest) * SCALE)
         share_of = 1.0 / (jnp.sum(weights, axis=-1, keepdims=True) + own)
-        weights = (weights * share_of).astype(jnp.bfloat16)
-        own = (own * share_of).astype(jnp.bfloat16).astype(jnp.float32)
+        weights = weights.astype(jnp.bfloat16)
+        own = own.astype(jnp.bfloat16).astype(jnp.float32)
         for i in range(CHUNK):
             parts = []
             for g in range(kv // 2):
@@ -192,7 +201,7 @@
                     weights[i, g * pair : (g + 1) * pair], values, preferred_element_type=jnp.float32
                 )
                 parts += [mixed[:share, :HEAD_DIM], mixed[share:, HEAD_DIM:]]
-            result = x[i] + jnp.concatenate(parts, axis=0) + own[i] * spread(fresh_v, i)
+            result = x[i] + (jnp.concatenate(parts, axis=0) + own[i] * spread(fresh_v, i)) * share_of[i]
             out_ref[c * CHUNK + i] = result.astype(jnp.bfloat16)
 
         @pl.when(me < sections - 1)
@@ -214,7 +223,8 @@
 
     @pl.when(me == 0)
     def _():
-        fill()
+        fill(0, k_pool)
+        fill(rows, v_pool)
         send_pieces(0, before)
 
     send_pieces(before, pieces)

time: 40.9 us -> 39.7 us (0.971); the launches traced: 40.1 us -> 39.5 us
  Pallas kernels: 39.5 us -> 38.9 us
    pallas_call x1, Pallas kernels: 36.9 us -> 36.3 us  [shards(): pl.pallas_call(functools.partial(relay_kernel, sections), out_shape=(jax....]
where the time goes in v4:
time: 39.7 us; the launch traced here: 39.5 us
  Pallas kernels  38.9 us (98%)
  between operations  0.64 us (2%)
    pallas_call x1, Pallas kernels, shards(): pl.pallas_call(functools.partial(relay_kernel, sections), out_shape=(jax....  36.3 us
    pallas_call x1, Pallas kernels, shards(): pl.pallas_call(finish_kernel, out_shape=(jax.ShapeDtypeStruct((1, rows, w...  2.61 us

profile of v4, /device:TPU:28, one launch (start us, length us, event | category | flops | bytes accessed | tf_op | source)
XLA Modules:
  0.0 39.5 jit_solution(10736553354411012291)
XLA Ops:
  0.6 36.3 %relay.1 = (bf16[32,32,128]{2,1,0:T(8,128)(2,1)}, bf16[64,16,512]{2,1,0:T(8,128)(2,1)}) custom-call(bf16[32,4096]{1,0:T(8,128)(2,1)} %x_hbm.1, bf16[256,16,512]{2,1,0:T(8,128)(2,1)} %bitcast.5, bf16[256,16,512]{2,1,0:T(8,128)(2,1)} %bitcast.6, bf16[32,512]{1,0:T(8,128)(2,1)} %bitcast.7, bf16[32,512]{1,0:T(8,128)(2,1)} %bitcast.8, bf16[1,4096]{1,0:T(2,128)(2,1)} %gain_hbm.1, ...), custom_call_target="tpu_custom_call" | custom-call | tf_op jit(solution)/shard_map/relay/pallas_call | solution.py:277
  36.9 2.6 %finish.1 = (bf16[1,32,4096]{2,1,0:T(8,128)(2,1)}, bf16[1,32,16,512]{3,2,1,0:T(8,128)(2,1)}, bf16[1,32,16,512]{3,2,1,0:T(8,128)(2,1)}) custom-call(bf16[32,32,128]{2,1,0:T(8,128)(2,1)} %get-tuple-element.5.x_hbm, bf16[64,16,512]{2,1,0:T(8,128)(2,1)} %get-tuple-element.6.pages_hbm), custom_call_target="tpu_custom_call" | custom-call | tf_op jit(solution)/shard_map/finish/pallas_call | solution.py:319
